TPU v7x, 32 devices: a whole 2x2x4 slice. The times are simulated.
32 devices in a mesh: slab: 4 (over y, core), sub: 8 (over z, x).
Axes of the slice: x: 2, y: 2, z: 4, core: 2. Of those that a mesh axis runs over, the one named last changes fastest.
Arguments:
- positions: float32 [3, 2097152], P(None, ('slab', 'sub')), may hold values from 0 to 32, as said below
- masses: float32 [2097152], P(('slab', 'sub')), may hold values from 0.001 to 0.01
- leaf_counts: int32 [8192], P(('slab', 'sub')), may hold values from 64 to 256, as said below
- send_leaves: int32 [32, 256], P(('slab', 'sub')), may hold values from 0 to 255, as said below
- send_parents: int32 [32, 64], P(('slab', 'sub')), may hold values from 0 to 31, as said below
- near_pairs: int32 [32, 3, 256], P(('slab', 'sub')), may hold values from -1 to 511, as said below
- far_pairs: int32 [32, 3, 1024], P(('slab', 'sub')), may hold values from -1 to 511, as said below
- parent_pairs: int32 [32, 3, 64], P(('slab', 'sub')), may hold values from -1 to 95, as said below
Outputs:
- field: float32 [4, 2097152], P(None, ('slab', 'sub'))
Inputs may be any that keep to these rules, and one draw needn't show every extreme that they name: `positions`: the coordinates of a body of leaf c on device (s, u) lie within one unit above that leaf's integer coordinates along each dimension. `leaf_counts`: every device has a leaf whose 256 slots are all used. `send_leaves`: within one direction of a row, the 64 leaves are different. `send_parents`: within one direction of a row, the 16 parent cells are different. `near_pairs`: row 0 is an own leaf, row 1 a leaf table entry or -1 for an unused entry (unused entries come last), row 2 the z image -1, 0 or 1 (0 where unused). Own pairs have a < b; no pair repeats; pairs are leaves at most one leaf apart along each dimension after the image. `far_pairs`: as near_pairs, for leaves whose squared separation after the image is 4 to 12 leaf units. `parent_pairs`: as near_pairs, for parent cells whose squared separation after the image is 2 parent units or more, with the parent table.
All inputs are finite; a program needn't handle non-finite values.
Results may differ from a plain program's by a relative error of at most 0.0003.
Values sent between devices are 32-bit elements; how exact they have to be, the bound alone decides.
No kernel may reach another device: no remote copies, remote signals or barrier semaphores. Data moves between devices by JAX's collectives and lax.ppermute only.
A program may use at most 320 MiB of HBM per device.

v0:
```python
import jax
import jax.numpy as jnp
from jax import lax
from jax.sharding import PartitionSpec as P

CX = 2
CY = 4
CZ = 32


tensor_offsets = (0, 1, 4, 13, 40, 121)
factorials = (1.0, 1.0, 2.0, 6.0, 24.0)
soft_square = 0.0025
slab_steps = (1, 0, 1, 1)
sub_steps = (0, 1, 1, -1)


def from_behind(value, axis, steps):
    count = lax.axis_size(axis)
    pairs = [(source, (source + steps) % count) for source in range(count)]
    return lax.ppermute(value, axis, pairs)


def outer_powers(offset):
    tail = offset.shape[1:]
    powers = [jnp.ones((1,) + tail, offset.dtype)]
    for degree in range(4):
        before = powers[-1]
        grown = before[:, None] * offset[None, :]
        powers.append(grown.reshape((before.shape[0] * 3,) + tail))
    return powers


def inverse_distance(vector):
    return 1.0 / jnp.sqrt(jnp.sum(vector * vector))


def jacobian_of(inner):

    def result(vector):
        values, pullback = jax.vjp(inner, vector)
        unit_rows = jnp.eye(values.shape[0], dtype=values.dtype)
        stacked = jax.vmap(pullback)(unit_rows)[0]
        return stacked.reshape(-1)

    return result


def derivative_tensors(separation):
    first_grad = jax.grad(inverse_distance)
    second_grad = jacobian_of(first_grad)
    third_grad = jacobian_of(second_grad)

    def single(vector):
        return (
            inverse_distance(vector).reshape(1),
            first_grad(vector),
            second_grad(vector),
            third_grad(vector),
            jacobian_of(third_grad)(vector),
        )

    return jax.vmap(single)(separation)


def mutual_locals(moments_a, moments_b, separation):
    tensors = derivative_tensors(separation)
    pair_count = separation.shape[0]
    locals_a = []
    locals_b = []
    for degree in range(5):
        summed_a = jnp.zeros((pair_count, 3**degree), jnp.float32)
        summed_b = jnp.zeros((pair_count, 3**degree), jnp.float32)
        for source in range(5 - degree):
            tensor_block = tensors[source + degree].reshape(pair_count, 3**source, 3**degree)
            piece_b = moments_b[:, tensor_offsets[source] : tensor_offsets[source + 1]]
            piece_a = moments_a[:, tensor_offsets[source] : tensor_offsets[source + 1]]
            summed_a = summed_a + (-1.0) ** source / factorials[source] * jnp.einsum(
                "pa,pab->pb", piece_b, tensor_block, precision=lax.Precision.HIGHEST
            )
            summed_b = summed_b + 1.0 / factorials[source] * jnp.einsum(
                "pa,pab->pb", piece_a, tensor_block, precision=lax.Precision.HIGHEST
            )
        locals_a.append(-summed_a)
        locals_b.append(-((-1.0) ** degree) * summed_b)
    return (jnp.concatenate(locals_a, 1), jnp.concatenate(locals_b, 1))


def shift_locals(parent_terms, offset):
    powers = outer_powers(offset)
    result = []
    for degree in range(5):
        summed = jnp.zeros((3**degree,) + offset.shape[1:], jnp.float32)
        for source in range(degree, 5):
            spacing = source - degree
            tensor_block = parent_terms[
                tensor_offsets[source] : tensor_offsets[source + 1]
            ].reshape((3**spacing, 3**degree) + offset.shape[1:])
            summed = (
                summed + jnp.sum(tensor_block * powers[spacing][:, None], 0) / factorials[spacing]
            )
        result.append(summed)
    return jnp.concatenate(result, 0)


def evaluate_locals(leaf_terms, powers):
    cell_count = leaf_terms.shape[1]
    potential = jnp.zeros(powers[0].shape[1:], jnp.float32)
    accel = jnp.zeros((3,) + powers[0].shape[1:], jnp.float32)
    for degree in range(5):
        tensor_block = leaf_terms[tensor_offsets[degree] : tensor_offsets[degree + 1]]
        potential = (
            potential + jnp.sum(tensor_block[:, :, None] * powers[degree], 0) / factorials[degree]
        )
        if degree < 4:
            upper = leaf_terms[tensor_offsets[degree + 1] : tensor_offsets[degree + 2]].reshape(
                3**degree, 3, cell_count
            )
            accel = (
                accel
                - jnp.sum(upper[:, :, :, None] * powers[degree][:, None], 0) / factorials[degree]
            )
    return jnp.concatenate([potential[None], accel], 0)


def pair_block(place_a, weight_a, place_b, weight_b):
    spacing = place_a[:, :, None] - place_b[:, None, :]
    inverse = lax.rsqrt(jnp.sum(spacing * spacing, 0) + soft_square)
    cubed = inverse * inverse * inverse
    potential_a = -jnp.sum(weight_b[None, :] * inverse, 1)
    potential_b = -jnp.sum(weight_a[:, None] * inverse, 0)
    accel_a = -jnp.sum(spacing * (weight_b[None, :] * cubed)[None], 2)
    accel_b = jnp.sum(spacing * (weight_a[:, None] * cubed)[None], 1)
    return (
        jnp.concatenate([potential_a[None], accel_a], 0),
        jnp.concatenate([potential_b[None], accel_b], 0),
    )


def self_block(places, weight_row):
    slot_count = weight_row.shape[0]
    spacing = places[:, :, None] - places[:, None, :]
    apart = lax.broadcasted_iota(jnp.int32, (slot_count, slot_count), 0) != lax.broadcasted_iota(
        jnp.int32, (slot_count, slot_count), 1
    )
    inverse = jnp.where(apart, lax.rsqrt(jnp.sum(spacing * spacing, 0) + soft_square), 0.0)
    cubed = inverse * inverse * inverse
    potential = -jnp.sum(weight_row[None, :] * inverse, 1)
    accel = -jnp.sum(spacing * (weight_row[None, :] * cubed)[None], 2)
    return jnp.concatenate([potential[None], accel], 0)


def self_work(body_rows):
    leaf_total = body_rows.shape[0]
    leaf_size = body_rows.shape[2]
    grouped = body_rows.reshape(leaf_total // 8, 8, 4, leaf_size)

    def self_one_group(bundle):
        return jax.vmap(self_block)(bundle[:, :3], bundle[:, 3])

    fields = lax.map(self_one_group, grouped)
    return fields.reshape(leaf_total, 4, leaf_size)


def near_work(table_bodies, pair_list):
    owned_ids = pair_list[0]
    partner_ids = jnp.maximum(pair_list[1], 0)
    active = pair_list[1] >= 0
    z_lift = pair_list[2].astype(jnp.float32) * CZ
    pair_count = owned_ids.shape[0]
    leaf_size = table_bodies.shape[2]

    def near_one_group(bundle):
        ids_a, ids_b, lifts, actives = bundle
        rows_a = jnp.take(table_bodies, ids_a, axis=0)
        rows_b = jnp.take(table_bodies, ids_b, axis=0)
        rows_b = rows_b.at[:, 2].add(lifts[:, None])
        part_a, part_b = jax.vmap(pair_block)(
            rows_a[:, :3], rows_a[:, 3], rows_b[:, :3], rows_b[:, 3]
        )
        keeper = actives[:, None, None]
        return (jnp.where(keeper, part_a, 0.0), jnp.where(keeper, part_b, 0.0))

    def shaped(values):
        return values.reshape(pair_count // 16, 16)

    part_a, part_b = lax.map(
        near_one_group, (shaped(owned_ids), shaped(partner_ids), shaped(z_lift), shaped(active))
    )
    part_a = part_a.reshape(pair_count, 4, leaf_size)
    part_b = part_b.reshape(pair_count, 4, leaf_size)
    summed = jnp.zeros(table_bodies.shape, jnp.float32)
    return summed.at[owned_ids].add(part_a).at[partner_ids].add(part_b)


def far_work(table_cells, pair_list):
    owned_ids = pair_list[0]
    partner_ids = jnp.maximum(pair_list[1], 0)
    active = pair_list[1] >= 0
    z_lift = pair_list[2].astype(jnp.float32) * CZ
    centre_a = jnp.take(table_cells[:, 121:], owned_ids, axis=0)
    centre_b = jnp.take(table_cells[:, 121:], partner_ids, axis=0)
    centre_b = centre_b.at[:, 2].add(z_lift)
    separation = jnp.where(active[:, None], centre_a - centre_b, 3.0)
    moments_a = jnp.take(table_cells[:, :121], owned_ids, axis=0)
    moments_b = jnp.take(table_cells[:, :121], partner_ids, axis=0)
    locals_a, locals_b = mutual_locals(moments_a, moments_b, separation)
    locals_a = jnp.where(active[:, None], locals_a, 0.0)
    locals_b = jnp.where(active[:, None], locals_b, 0.0)
    summed = jnp.zeros((table_cells.shape[0], 121), jnp.float32)
    return summed.at[owned_ids].add(locals_a).at[partner_ids].add(locals_b)


def geometry(slab_at, sub_at):
    leaf_ids = jnp.arange(CX * CY * CZ, dtype=jnp.int32)
    cell_x = leaf_ids // (CY * CZ)
    cell_y = leaf_ids // CZ % CY
    cell_z = leaf_ids % CZ
    base_x = slab_at * CX
    base_y = sub_at * CY
    centres = jnp.stack([base_x + cell_x, base_y + cell_y, cell_z]).astype(jnp.float32) + 0.5
    half_y = CY // 2
    half_z = CZ // 2
    parent_of = (cell_x // 2 * half_y + cell_y // 2) * half_z + cell_z // 2
    parent_ids = jnp.arange(CX // 2 * half_y * half_z, dtype=jnp.int32)
    parent_x = parent_ids // (half_y * half_z)
    parent_y = parent_ids // half_z % half_y
    parent_z = parent_ids % half_z
    parent_centres = (
        jnp.stack([base_x + 2 * parent_x, base_y + 2 * parent_y, 2 * parent_z]).astype(jnp.float32)
        + 1.0
    )
    return (centres, parent_centres, parent_of)


def image_shift(slab_at, sub_at, slab_count, sub_count):
    rows_out = []
    for direction in range(4):
        reach_x = slab_at + slab_steps[direction]
        reach_y = sub_at + sub_steps[direction]
        jump_x = (reach_x - reach_x % slab_count) * CX
        jump_y = (reach_y - reach_y % sub_count) * CY
        rows_out.append(jnp.stack([jump_x, jump_y, jnp.zeros_like(jump_x)]))
    return jnp.stack(rows_out).astype(jnp.float32)


def device_front(positions, masses, leaf_counts, send_leaves, send_parents, slab_at, sub_at):
    leaf_total = leaf_counts.shape[0]
    leaf_size = masses.shape[0] // leaf_total
    places = positions.reshape(3, leaf_total, leaf_size)
    filled = lax.broadcasted_iota(jnp.int32, (leaf_total, leaf_size), 1) < leaf_counts[:, None]
    weights = jnp.where(filled, masses.reshape(leaf_total, leaf_size), 0.0)
    centres, parent_centres, parent_of = geometry(slab_at, sub_at)
    parent_total = parent_centres.shape[1]
    leaf_powers = outer_powers(places - centres[:, :, None])
    moments = jnp.sum(jnp.concatenate(leaf_powers, 0) * weights[None], 2)
    parent_powers = jnp.concatenate(
        outer_powers(places - jnp.take(parent_centres, parent_of, axis=1)[:, :, None]), 0
    )
    per_leaf = jnp.sum(parent_powers * weights[None], 2)
    belongs = (parent_of[:, None] == jnp.arange(parent_total, dtype=jnp.int32)[None, :]).astype(
        jnp.float32
    )
    parent_moments = jnp.dot(per_leaf, belongs, precision=lax.Precision.HIGHEST)
    body_rows = jnp.concatenate([places, weights[None]], 0).transpose(1, 0, 2)
    leaf_rows = jnp.concatenate([moments, centres], 0).T
    parent_rows = jnp.concatenate([parent_moments, parent_centres], 0).T
    out_bodies = jnp.take(body_rows, send_leaves, axis=0).reshape(4, -1)
    out_leaf = jnp.take(leaf_rows, send_leaves, axis=0).reshape(4, -1)
    out_parent = jnp.take(parent_rows, send_parents, axis=0).reshape(4, -1)
    outgoing = jnp.concatenate([out_bodies, out_leaf, out_parent], 1)
    return (
        filled,
        leaf_powers,
        body_rows,
        leaf_rows,
        parent_rows,
        centres,
        parent_centres,
        parent_of,
        send_leaves,
        send_parents,
        outgoing,
    )


def device_middle(
    body_rows, leaf_rows, parent_rows, incoming, image, near_list, far_list, parent_list
):
    leaf_total = body_rows.shape[0]
    leaf_size = body_rows.shape[2]
    parent_total = parent_rows.shape[0]
    slots = leaf_total // 4
    parent_slots = parent_total // 2
    cut_a = 4 * slots * leaf_size
    cut_b = cut_a + 124 * slots
    body_lift = jnp.concatenate([image, jnp.zeros((4, 1), jnp.float32)], 1)
    cell_lift = jnp.concatenate([jnp.zeros((4, 121), jnp.float32), image], 1)
    in_bodies = incoming[:, :cut_a].reshape(4, slots, 4, leaf_size) + body_lift[:, None, :, None]
    in_leaf = incoming[:, cut_a:cut_b].reshape(4, slots, 124) + cell_lift[:, None, :]
    in_parent = incoming[:, cut_b:].reshape(4, parent_slots, 124) + cell_lift[:, None, :]
    table_bodies = jnp.concatenate([body_rows, in_bodies.reshape(4 * slots, 4, leaf_size)], 0)
    table_leaf = jnp.concatenate([leaf_rows, in_leaf.reshape(4 * slots, 124)], 0)
    table_parent = jnp.concatenate([parent_rows, in_parent.reshape(4 * parent_slots, 124)], 0)
    near_table = near_work(table_bodies, near_list)
    local_near = near_table[:leaf_total] + self_work(body_rows)
    leaf_table = far_work(table_leaf, far_list)
    parent_table = far_work(table_parent, parent_list)
    back_bodies = near_table[leaf_total:].reshape(4, -1)
    back_leaf = leaf_table[leaf_total:].reshape(4, -1)
    back_parent = parent_table[parent_total:].reshape(4, -1)
    returning = jnp.concatenate([back_bodies, back_leaf, back_parent], 1)
    return (returning, local_near, leaf_table[:leaf_total], parent_table[:parent_total])


def device_back(
    local_near,
    leaf_terms,
    parent_terms,
    arrived,
    flat_leaf,
    flat_parent,
    leaf_powers,
    centres,
    parent_centres,
    parent_of,
    filled,
):
    leaf_size = local_near.shape[2]
    slots = flat_leaf.shape[0] // 4
    cut_a = 4 * slots * leaf_size
    cut_b = cut_a + 121 * slots
    got_bodies = arrived[:, :cut_a].reshape(4 * slots, 4, leaf_size)
    got_leaf = arrived[:, cut_a:cut_b].reshape(4 * slots, 121)
    got_parent = arrived[:, cut_b:].reshape(-1, 121)
    local_near = local_near.at[flat_leaf].add(got_bodies)
    leaf_terms = leaf_terms.at[flat_leaf].add(got_leaf)
    parent_terms = parent_terms.at[flat_parent].add(got_parent)
    leaf_columns = leaf_terms.T + shift_locals(
        jnp.take(parent_terms, parent_of, axis=0).T,
        centres - jnp.take(parent_centres, parent_of, axis=1),
    )
    result = evaluate_locals(leaf_columns, leaf_powers) + local_near.transpose(1, 0, 2)
    result = jnp.where(filled[None], result, 0.0)
    return result.reshape(4, -1)


def on_device(
    positions, masses, leaf_counts, send_leaves, send_parents, near_pairs, far_pairs, parent_pairs
):
    slab_count = lax.axis_size("slab")
    sub_count = lax.axis_size("sub")
    slab_at = lax.axis_index("slab")
    sub_at = lax.axis_index("sub")
    parts = device_front(
        positions, masses, leaf_counts, send_leaves[0], send_parents[0], slab_at, sub_at
    )
    outgoing = parts[10]
    image = image_shift(slab_at, sub_at, slab_count, sub_count)
    slab_moved = from_behind(jnp.stack([outgoing[0], outgoing[2], outgoing[3]]), "slab", -1)
    rising = from_behind(jnp.stack([outgoing[1], slab_moved[1]]), "sub", -1)
    falling = from_behind(slab_moved[2], "sub", 1)
    incoming = jnp.stack([slab_moved[0], rising[0], rising[1], falling])
    returning, local_near, leaf_terms, parent_terms = device_middle(
        parts[2], parts[3], parts[4], incoming, image, near_pairs[0], far_pairs[0], parent_pairs[0]
    )
    back_rise = from_behind(jnp.stack([returning[1], returning[2]]), "sub", 1)
    back_fall = from_behind(returning[3], "sub", -1)
    back_slab = from_behind(jnp.stack([returning[0], back_rise[1], back_fall]), "slab", 1)
    arrived = jnp.stack([back_slab[0], back_rise[0], back_slab[1], back_slab[2]])
    return device_back(
        local_near,
        leaf_terms,
        parent_terms,
        arrived,
        parts[8],
        parts[9],
        parts[1],
        parts[5],
        parts[6],
        parts[7],
        parts[0],
    )


def solution(mesh):
    return jax.shard_map(
        on_device,
        mesh=mesh,
        in_specs=(
            P(None, ("slab", "sub")),
            P(("slab", "sub")),
            P(("slab", "sub")),
            P(("slab", "sub"), None),
            P(("slab", "sub"), None),
            P(("slab", "sub"), None, None),
            P(("slab", "sub"), None, None),
            P(("slab", "sub"), None, None),
        ),
        out_specs=P(None, ("slab", "sub")),
        check_vma=False,
    )
```

profile of v0, /device:TPU:0, one launch (start us, length us, event | category | flops | bytes accessed | tf_op | source)
XLA Modules:
  0.0 852.1 jit_solution(13136839889909522151)
XLA Ops:
  31.1 10.3 %broadcast_multiply_fusion = f32[27,3,256,256]{3,2,1,0:T(8,128)} fusion(f32[3,256,256]{2,1,0:T(8,128)S(1)} %copy-done.5, f32[27,256,256]{2,1,0:T(8,128)} %bitcast.24), kind=kLoop, calls=%fused_computation.79 | loop fusion | flops 5308416 | bytes 29097984 | tf_op jit(solution)/shard_map/mul | solution.py:29
  41.4 6.7 constant_dynamic-update-slice_fusion.5
  48.1 10.6 %constant_dynamic-update-slice_fusion = f32[121,256,256]{2,1,0:T(8,128)} fusion(f32[121,256,256]{2,1,0:T(8,128)} %constant_dynamic-update-slice_fusion.1, f32[81,256,256]{2,1,0:T(8,128)S(1)} %bitcast.277), kind=kLoop, calls=%fused_computation.354 | loop fusion | bytes 42467328 | tf_op jit(solution)/shard_map/concatenate | solution.py:256
  61.2 7.3 constant_dynamic-update-slice_fusion.4
  68.6 21.9 %multiply_reduce_fusion.4 = (f32[121,256]{1,0:T(8,128)S(1)}, f32[121,256]{1,0:T(8,128)S(1)}) fusion(f32[121,256,256]{2,1,0:T(8,128)} %constant_dynamic-update-slice_fusion, f32[256,256]{1,0:T(8,128)S(1)} %broadcast_select_fusion.7, f32[121,256,256]{2,1,0:T(8,128)} %constant_dynamic-update-slice_fusion.4), kind=kLoop, calls=%fused_computation.75 | loop fusion | flops 31657472 | bytes 63948800 | tf_op jit(solution)/shard_map/reduce_sum | solution.py:256
  112.2 166.9 %while.28 = (s32[]{:T(128)}, f32[32,8,4,256]{3,2,1,0:T(4,128)}, f32[32,8,4,256]{3,1,0,2:T(8,128)}, s32[]{:T(128)}) while((s32[]{:T(128)}, f32[32,8,4,256]{3,2,1,0:T(4,128)}, f32[32,8,4,256]{3,1,0,2:T(8,128)}, s32[]{:T(128)}) %tuple.289), condition=%wide.region_117.124_spmd, body=%wide.region_113.123_spmd.sunk | while | flops 12656642 | bytes 8938041 | solution.py:161
  297.1 11.5 %collective-permute-done.2 = f32[75456]{0:T(1024)S(1)} collective-permute-done((f32[75456]{0:T(1024)}, f32[75456]{0:T(1024)S(1)}, u32[]{:S(2)}, u32[]{:S(2)}) %collective-permute-start.2) | collective-permute-done | bytes 301856 | tf_op jit(solution)/shard_map/ppermute | solution.py:21
  347.5 5.9 multiply_reduce_fusion.17
  431.0 6.2 scatter_custom_fusion
  437.3 6.4 scatter_fusion
  448.9 272.0 %while.27 = (s32[]{:T(128)}, f32[16,16,4,256]{3,2,1,0:T(4,128)S(1)}, f32[16,16,4,256]{3,2,1,0:T(4,128)S(1)}, pred[16,16]{1,0:T(8,128)(4,1)}, s32[16,16]{1,0:T(8,...) while((s32[]{:T(128)}, ...), condition=%wide.region_52.57_spmd, body=%wide.region_46.56_spmd.sunk | while | flops 33646784 | bytes 26781088 | solution.py:187
  459.6 5.5 fusion.112
  476.6 5.5 fusion.112
  510.6 5.5 fusion.112
  561.5 5.5 fusion.112
  612.5 5.5 fusion.112
  663.5 5.5 fusion.112
  697.5 5.5 fusion.112
  722.2 8.8 %scatter_fusion.1 = f32[512,4,256]{2,1,0:T(4,128)S(1)} fusion(f32[512,4,256]{2,1,0:T(4,128)S(1)} %broadcast_in_dim.316, s32[256]{0:T(256)S(1)} %bitcast.314, f32[256,4,256]{2,1,0:T(4,128)S(1)} %bitcast.296), kind=kCustom, calls=%fused_computation.17 | custom fusion | flops 262144 | bytes 3146752 | tf_op jit(solution)/shard_map/scatter-add | solution.py:193
  731.0 19.4 %scatter_fusion.2 = f32[512,4,256]{2,1,0:T(4,128)S(1)} fusion(f32[512,4,256]{2,1,0:T(4,128)S(1)} %scatter_fusion.1, s32[256]{0:T(256)S(1)} %bitcast.313, f32[256,4,256]{2,1,0:T(4,128)} %bitcast.297), kind=kCustom, calls=%fused_computation.18 | custom fusion | flops 262144 | bytes 3146752 | tf_op jit(solution)/shard_map/scatter-add | solution.py:193
  777.1 17.5 %collective-permute-done.4 = f32[75216]{0:T(1024)S(1)} collective-permute-done((f32[75216]{0:T(1024)S(1)}, f32[75216]{0:T(1024)S(1)}, u32[]{:S(2)}, u32[]{:S(2)}) %collective-permute-start.4) | collective-permute-done | bytes 300896 | tf_op jit(solution)/shard_map/ppermute | solution.py:21
  798.5 13.6 %collective-permute-done.5 = f32[3,75216]{1,0:T(4,128)S(1)} collective-permute-done((f32[3,75216]{1,0:T(4,128)S(1)}, f32[3,75216]{1,0:T(4,128)S(1)}, u32[]{:S(2)}, u32[]{:S(2)}) %collective-permute-start.5) | collective-permute-done | bytes 902624 | tf_op jit(solution)/shard_map/ppermute | solution.py:21
  831.2 7.0 multiply_reduce_fusion.6
  838.3 8.8 %scatter_fusion.5 = f32[256,4,256]{2,1,0:T(4,128)S(1)} fusion(f32[256,4,256]{2,1,0:T(4,128)S(1)} %copy-done.6, s32[256]{0:T(256)S(1)} %bitcast.310, f32[256,4,256]{2,1,0:T(4,128)S(1)} %copy-done.14), kind=kCustom, calls=%fused_computation.23 | custom fusion | flops 262144 | bytes 3146752 | tf_op jit(solution)/shard_map/scatter-add | solution.py:336
  (1504 shorter events, 643.5 us)
Async XLA Ops:
  4.8 88.2 %copy-start.153 = (s32[64]{0:T(128)}, s32[64]{0:T(128)S(1)}, u32[]{:S(2)}) copy-start(s32[64]{0:T(128)S(1)} %fusion.78) | copy-start | bytes 772
  41.4 17.3 %slice-start = ((s8[21233664]{0:T(1024)(128)(4,1)}), s8[262144]{0:T(1024)(128)(4,1)S(1)}, s32[]{:S(2)}) async-start(s8[21233664]{0:T(1024)(128)(4,1)} %bitcast.278), calls=%async_computation | async-start | bytes 524288
  41.4 17.3 %slice-start.1 = ((s8[21233664]{0:T(1024)(128)(4,1)}), s8[4194304]{0:T(1024)(128)(4,1)S(1)}, s32[]{:S(2)}) async-start(s8[21233664]{0:T(1024)(128)(4,1)} %bitcast.278), calls=%async_computation.1 | async-start | bytes 8388608
  68.6 22.0 %copy-start.40 = (f32[3,256]{0,1:T(8,128)S(1)}, f32[3,256]{0,1:T(8,128)}, u32[]{:S(2)}) copy-start(f32[3,256]{0,1:T(8,128)} %copy.826) | copy-start | bytes 9220
  68.6 23.8 %copy-start.157 = (s32[1,3,64]{2,0,1:T(1,128)S(1)}, s32[1,3,64]{2,0,1:T(1,128)}, u32[]{:S(2)}) copy-start(s32[1,3,64]{2,0,1:T(1,128)} %param.37) | copy-start | bytes 2308
  105.8 174.8 %collective-permute-start = (f32[3,75456]{1,0:T(4,128)}, f32[3,75456]{1,0:T(4,128)}, u32[]{:S(2)}, u32[]{:S(2)}) collective-permute-start(f32[3,75456]{1,0:T(4,128)} %fusion.14), channel_id=1, source_target_pairs={{0,24},{8,0},{16,8},{24,16},{1,25},{9,1},{17,9},{25,17},{2,26},{10... | collective-permute-start | bytes 2716424 | tf_op jit(solution)/shard_map/ppermute | solution.py:21
  108.2 187.6 %copy-start.88 = (s32[1,1,1024]{2,0,1:T(1,128)}, s32[1,1,1024]{2,0,1:T(1,128)S(1)}, u32[]{:S(2)}) copy-start(s32[1,1,1024]{2,0,1:T(1,128)S(1)} %get-tuple-element.474) | copy-start | bytes 12292
  108.2 226.3 %copy-start.128 = (pred[1024]{0:T(1024)(128)(4,1)}, pred[1024]{0:T(1024)(128)(4,1)S(1)}, u32[]{:S(2)}) copy-start(pred[1024]{0:T(1024)(128)(4,1)S(1)} %compare_reduce_fusion) | copy-start | bytes 3076
  108.2 227.0 %copy-start.104 = (f32[3,3]{1,0:T(4,128)}, f32[3,3]{1,0:T(4,128)S(1)}, u32[]{:S(2)}) copy-start(f32[3,3]{1,0:T(4,128)S(1)} %fusion.65) | copy-start | bytes 112
  108.3 290.7 %copy-start.62 = (f32[3,3]{1,0:T(4,128)}, f32[3,3]{1,0:T(4,128)S(1)}, u32[]{:S(2)}) copy-start(f32[3,3]{1,0:T(4,128)S(1)} %fusion.52) | copy-start | bytes 112
  111.6 235.8 %copy-start.64 = (f32[27,9,3]{0,2,1:T(4,128)}, f32[27,9,3]{0,2,1:T(4,128)S(1)}, u32[]{:S(2)}) copy-start(f32[27,9,3]{0,2,1:T(4,128)S(1)} %get-tuple-element.293) | copy-start | bytes 8752
  286.8 22.0 %collective-permute-start.1 = (f32[2,75456]{1,0:T(2,128)}, f32[2,75456]{1,0:T(2,128)S(1)}, u32[]{:S(2)}, u32[]{:S(2)}) collective-permute-start(f32[2,75456]{1,0:T(2,128)} %fusion.19), channel_id=1, source_target_pairs={{0,7},{1,0},{2,1},{3,2},{4,3},{5,4},{6,5},{7,6},{8,15},{9,8},{10,9... | collective-permute-start | bytes 1810952 | tf_op jit(solution)/shard_map/ppermute | solution.py:21
  292.2 22.7 %copy-start.110 = (f32[4,124]{1,0:T(4,128)}, f32[4,124]{1,0:T(4,128)S(1)}, u32[]{:S(2)}) copy-start(f32[4,124]{1,0:T(4,128)S(1)} %concatenate.109) | copy-start | bytes 5956
  295.8 12.9 %collective-permute-start.2 = (f32[75456]{0:T(1024)}, f32[75456]{0:T(1024)S(1)}, u32[]{:S(2)}, u32[]{:S(2)}) collective-permute-start(f32[75456]{0:T(1024)} %get-tuple-element.406), channel_id=1, source_target_pairs={{0,1},{1,2},{2,3},{3,4},{4,5},{5,6},{6,7},{7,0},{8,9},{9,10},{10,1... | collective-permute-start | bytes 905480 | tf_op jit(solution)/shard_map/ppermute | solution.py:21
  378.3 18.2 %copy-start.65 = (f32[27,9,3]{0,2,1:T(4,128)S(1)}, f32[27,9,3]{0,2,1:T(4,128)}, u32[]{:S(2)}) copy-start(f32[27,9,3]{0,2,1:T(4,128)} %copy-done.64) | copy-start | bytes 8752
  383.0 20.0 %copy-start.78 = (f32[64,3]{0,1:T(4,128)}, f32[64,3]{0,1:T(4,128)S(1)}, u32[]{:S(2)}) copy-start(f32[64,3]{0,1:T(4,128)S(1)} %get-tuple-element.384) | copy-start | bytes 2308
  396.4 16.2 %copy-start.22 = (f32[1024,27]{1,0:T(8,128)S(1)}, f32[1024,27]{1,0:T(8,128)}, u32[]{:S(2)}) copy-start(f32[1024,27]{1,0:T(8,128)} %slice.493) | copy-start | bytes 331780
  399.3 18.3 %copy-start.23 = (f32[1024,81]{1,0:T(8,128)S(1)}, f32[1024,81]{1,0:T(8,128)}, u32[]{:S(2)}) copy-start(f32[1024,81]{1,0:T(8,128)} %slice.494) | copy-start | bytes 995332
  448.9 273.3 %copy-start.148 = (s32[256,1]{0,1:T(1,128)S(1)}, s32[256,1]{0,1:T(1,128)}, u32[]{:S(2)}) copy-start(s32[256,1]{0,1:T(1,128)} %compare_select_fusion.6) | copy-start | bytes 3076
  765.1 31.1 %copy-start.15 = (f32[1,3,256,256]{3,2,1,0:T(8,128)S(1)}, f32[1,3,256,256]{3,2,1,0:T(8,128)}, u32[]{:S(2)}) copy-start(f32[1,3,256,256]{3,2,1,0:T(8,128)} %get-tuple-element.482) | copy-start | bytes 2359300
  768.5 29.3 %copy-start.127 = (s32[256]{0:T(256)S(1)}, s32[256]{0:T(256)}, u32[]{:S(2)}) copy-start(s32[256]{0:T(256)} %param.32) | copy-start | bytes 3076
  768.5 26.4 %collective-permute-start.3 = (f32[2,75216]{1,0:T(2,128)S(1)}, f32[2,75216]{1,0:T(2,128)S(1)}, u32[]{:S(2)}, u32[]{:S(2)}) collective-permute-start(f32[2,75216]{1,0:T(2,128)S(1)} %stack.108), channel_id=1, source_target_pairs={{0,1},{1,2},{2,3},{3,4},{4,5},{5,6},{6,7},{7,0},{8,9},{9,10},{10,1... | collective-permute-start | bytes 1805192 | tf_op jit(solution)/shard_map/ppermute | solution.py:21
  772.5 22.1 %collective-permute-start.4 = (f32[75216]{0:T(1024)S(1)}, f32[75216]{0:T(1024)S(1)}, u32[]{:S(2)}, u32[]{:S(2)}) collective-permute-start(f32[75216]{0:T(1024)S(1)} %get-tuple-element.409), channel_id=1, source_target_pairs={{0,7},{1,0},{2,1},{3,2},{4,3},{5,4},{6,5},{7,6},{8,15},{9,8},{10,9... | collective-permute-start | bytes 902600 | tf_op jit(solution)/shard_map/ppermute | solution.py:21
  796.1 15.9 %collective-permute-start.5 = (f32[3,75216]{1,0:T(4,128)S(1)}, f32[3,75216]{1,0:T(4,128)S(1)}, u32[]{:S(2)}, u32[]{:S(2)}) collective-permute-start(f32[3,75216]{1,0:T(4,128)S(1)} %pad_maximum_fusion.3), channel_id=1, source_target_pairs={{0,8},{8,16},{16,24},{24,0},{1,9},{9,17},{17,25},{25,1},{2,10},{10... | collective-permute-start | bytes 2707784 | tf_op jit(solution)/shard_map/ppermute | solution.py:21
  (148 other events, 887.3 us)
where the time goes:
time: 868 us; the launch traced here: 852 us
  other arithmetic  502 us (58%)
  local copies, waits for them, and re-layouts  283 us (33%)
  waiting for transfers between devices  42.6 us (5%)
  starting transfers between devices  14.7 us (2%)
    reduce_sum x16, other arithmetic, pair_block(): accel_b = jnp.sum(spacing * (weight_a[:, None] * cubed)[None], 1)  88.4 us
    reduce_sum x32, other arithmetic, self_block(): accel = -jnp.sum(spacing * (weight_row[None, :] * cubed)[None], 2)  59.8 us
    ppermute x6, waiting for transfers between devices, from_behind(): return lax.ppermute(value, axis, pairs)  42.6 us
    reduce_sum x32, other arithmetic, self_block(): jnp.sum(spacing * spacing, 0) + soft_square  35.4 us
    reduce_sum x16, other arithmetic, pair_block(): inverse = lax.rsqrt(jnp.sum(spacing * spacing, 0) + soft_square)  35.2 us
    unnamed x356, local copies, waits for them, and re-layouts  34.9 us
    gather x16, local copies, waits for them, and re-layouts, near_one_group(): rows_a = jnp.take(table_bodies, ids_a, axis=0)  34.9 us
    gather x16, local copies, waits for them, and re-layouts, near_one_group(): rows_b = jnp.take(table_bodies, ids_b, axis=0)  34.9 us
  transfers between devices with their start and end apart: 6, of which 3 were waited for; matrix products, arithmetic and copies ran while one was open for 21% of the time, Pallas kernels for 0%

commit v1 on v0

v1 whole, which is shorter than its diff:
```python
import functools
import math

import jax
import jax.numpy as jnp
import numpy as np
from jax import lax
from jax.experimental import pallas as pl
from jax.experimental.pallas import tpu as pltpu
from jax.sharding import PartitionSpec as P

CX = 2
CY = 4
CZ = 32

soft_square = 0.0025
slab_steps = (1, 0, 1, 1)
sub_steps = (0, 1, 1, -1)

LEAVES = CX * CY * CZ
PARENTS = LEAVES // 8
SLOTS = LEAVES // 4
PSLOTS = PARENTS // 2
HALF = 128
LEAF = 2 * HALF
BODY_ROWS = 8 * SLOTS
PACK_ROWS = BODY_ROWS + SLOTS + PSLOTS
GROUP = 8
bf16 = jnp.bfloat16
f32 = jnp.float32
i32 = jnp.int32

MULTI = [
    (i, j, n - i - j) for n in range(5) for i in range(n, -1, -1) for j in range(n - i, -1, -1)
]
PLACE = {alpha: at for at, alpha in enumerate(MULTI)}
TERMS = len(MULTI)
CENTRE = TERMS
FEATS = 40
OWN = LEAVES + PARENTS
ENTRIES = 640
FAR_BLOCKS = 9


def fact(alpha):
    return math.prod(math.factorial(a) for a in alpha)


def added(alpha, beta):
    return tuple(a + b for a, b in zip(alpha, beta))


def taken(alpha, beta):
    return tuple(a - b for a, b in zip(alpha, beta))


def octant(at):
    return tuple(0.5 if bit else -0.5 for bit in (at >> 2 & 1, at >> 1 & 1, at & 1))


def power(delta, alpha):
    return math.prod(d**a for d, a in zip(delta, alpha))


def shift_matrices():
    up = np.zeros((8, 128, 128), np.float32)
    down = np.zeros((8, 128, 128), np.float32)
    for at in range(8):
        delta = octant(at)
        for alpha in MULTI:
            for beta in MULTI:
                rest = taken(alpha, beta)
                if min(rest) < 0:
                    continue
                choose = math.prod(math.comb(a, b) for a, b in zip(alpha, beta))
                up[at, PLACE[beta], PLACE[alpha]] = choose * power(delta, rest)
                down[at, PLACE[alpha], PLACE[beta]] = power(delta, rest) / fact(rest)
    return up.reshape(8 * 128, 128), down.transpose(1, 0, 2).reshape(128, 8 * 128)


UP, DOWN = shift_matrices()


def row_ids(shape):
    return lax.broadcasted_iota(i32, shape, 0)


def lane_ids(shape):
    return lax.broadcasted_iota(i32, shape, 1)


def monomials(x, y, z):
    table = {(0, 0, 0): None}
    axes = (x, y, z)
    for alpha in MULTI[1:]:
        lead = max(axis for axis in range(3) if alpha[axis])
        less = tuple(a - (axis == lead) for axis, a in enumerate(alpha))
        table[alpha] = axes[lead] if table[less] is None else table[less] * axes[lead]
    return table


def split3(value):
    high = value.astype(bf16).astype(f32)
    rest = value - high
    middle = rest.astype(bf16).astype(f32)
    return high, middle, rest - middle


def spread(tile):
    row = row_ids((8, HALF))
    turned = pltpu.roll(tile, 4, 0)
    low = row < 4
    return jnp.concatenate([jnp.where(low, tile, turned), jnp.where(low, turned, tile)], 1)


def fold(field):
    row = row_ids((8, HALF))
    return jnp.where(row < 4, field[:, :HALF], pltpu.roll(field[:, HALF:], 4, 0))


def offset_rows(ox, oy, oz):
    row = row_ids((8, LEAF)) & 3
    return jnp.where(row == 1, ox, jnp.where(row == 2, oy, jnp.where(row == 3, oz, 0.0)))


def features(tile, offset, as_row, as_column, as_weight):
    wide = spread(tile)
    row = row_ids((8, LEAF))
    first = (row & 3) == 0
    low = row < 4
    weight = jnp.broadcast_to(wide[0:1], (8, LEAF))
    x = jnp.where(first, 0.0, wide + offset)
    square = x * x
    pairwise = square + pltpu.roll(square, 1, 0)
    q = pairwise + pltpu.roll(pairwise, 2, 0)
    y = jnp.where(first, q, x)
    zero = jnp.zeros((8, LEAF), f32)
    out = [x, q]
    if as_row:
        h, m, l = split3(y)
        part_a = jnp.where(row == 4, m, h)
        part_b = jnp.where(row == 0, l, jnp.where(row == 4, 1.0, m))
        part_c = jnp.where(first, 1.0, jnp.where(low, h, l))
        out.append(jnp.concatenate([part_a, part_b, part_c, zero], 0).astype(bf16))
    if as_column:
        h, m, l = split3(jnp.where(first, q + soft_square, x * -2.0))
        mixed = jnp.where(low, h, m)
        part_a = jnp.where(first, 1.0, mixed)
        part_b = jnp.where(row == 0, 1.0, jnp.where(row == 4, h, mixed))
        part_c = jnp.where(row == 0, m, jnp.where(row == 4, l, jnp.where(low, l, h)))
        out.append(jnp.concatenate([part_a, part_b, part_c, zero], 0).astype(bf16))
    if as_weight:
        heavy = jnp.where(low, y, 1.0) * weight
        out.append(jnp.concatenate(list(split3(heavy)) + [zero], 0).astype(bf16))
    return out


def field_of(sums, x, q):
    total = sums[0:8] + sums[8:16] + sums[16:24]
    row = row_ids((8, LEAF))
    first = (row & 3) == 0
    plain = pltpu.roll(total, 4, 0)
    inner = total - jnp.where(first, q - soft_square, x) * plain
    along = x * inner
    dots = along[1:2] + along[2:3] + along[3:4]
    return fold(jnp.where(row == 0, 2.0 * dots - inner, inner))


def cubes(row_part, column_part):
    square = lax.dot_general(
        row_part, column_part, (((0,), (0,)), ((), ())), preferred_element_type=f32
    )
    inverse = lax.rsqrt(square)
    return inverse * inverse * inverse


def padded(sums):
    lanes = sums.shape[1]
    if lanes == LEAF:
        return sums
    return jnp.concatenate([sums, jnp.zeros((sums.shape[0], LEAF - lanes), f32)], 1)


def pipeline(count, group, early, late):
    @pl.when(count > 0)
    def _():
        for u in range(group):
            early(0, 0, u)

        def step(k, carry):
            for slot in range(2):
                done = []
                for u in range(group):
                    done.append(late(2 * k + slot, slot, u))
                    early(2 * k + slot + 1, 1 - slot, u)
                for store in done:
                    store()
            return carry

        lax.fori_loop(0, (count + 2 * group - 1) // (2 * group), step, 0)


def leaf_centre(place, leaf):
    return (
        -(place[0] + leaf // (CY * CZ)).astype(f32) - 0.5,
        -(place[1] + leaf // CZ % CY).astype(f32) - 0.5,
        -(leaf % CZ).astype(f32) - 0.5,
    )


def self_loop(words, at, count, group, size, place, bodies, field, scratch):
    cube_refs, weight_refs, spot_refs = scratch

    def early(k, slot, u):
        leaf = words[at, k * group + u]
        x, q, rows, columns, weights = features(
            bodies[leaf], offset_rows(*leaf_centre(place, leaf & (LEAVES - 1))), True, True, True
        )
        c = cubes(rows[:, :size], columns[:, :size])
        c = jnp.where(row_ids((size, size)) == lane_ids((size, size)), 0.0, c)
        high = c.astype(bf16)
        cube_refs[slot][u, :size, :size] = high
        cube_refs[slot][u, size : 2 * size, :size] = (c - high.astype(f32)).astype(bf16)
        weight_refs[slot][u, :, :size] = weights[:, :size]
        spot_refs[slot][u, 0] = x
        spot_refs[slot][u, 1] = q

    def late(k, slot, u):
        leaf = words[at, k * group + u]
        w = weight_refs[slot][u, :, :size]
        sums = jnp.dot(
            jnp.concatenate([w, w], 1),
            cube_refs[slot][u, : 2 * size, :size],
            preferred_element_type=f32,
        )
        result = field_of(padded(sums), spot_refs[slot][u, 0], spot_refs[slot][u, 1])

        def store():
            field[leaf] = field[leaf] + result

        return store

    pipeline(count, group, early, late)


def pair_loop(words, at, count, group, size, place, bodies, others, field, other_field, scratch):
    cube_refs, row_refs, column_refs, spot_refs = scratch
    turned = (((1,), (1,)), ((), ()))

    def unpack(k, u):
        word = words[at, k * group + u]
        return word & 511, word >> 9 & 511, word >> 18 & 1, (word >> 19 & 3) - 1, word >> 21 & 7

    def early(k, slot, u):
        row_leaf, column_leaf, swapped, lift, way = unpack(k, u)
        frame = jnp.where(swapped == 1, column_leaf, row_leaf) & (LEAVES - 1)
        cx, cy, cz = leaf_centre(place, frame)
        raised = (lift * CZ).astype(f32)
        swap = (swapped == 1).astype(f32)
        jump_x = place[2 + 2 * way].astype(f32)
        jump_y = place[3 + 2 * way].astype(f32)
        row_offset = offset_rows(cx, cy, cz + swap * raised)
        column_offset = offset_rows(cx + jump_x, cy + jump_y, cz + (1.0 - swap) * raised)
        xr, qr, rows, row_weights = features(bodies[row_leaf], row_offset, True, False, True)
        xc, qc, columns, column_weights = features(
            others[column_leaf], column_offset, False, True, True
        )
        c = cubes(rows[:, :size], columns)
        high = c.astype(bf16)
        cube_refs[slot][u, :size] = high
        cube_refs[slot][u, size : 2 * size] = (c - high.astype(f32)).astype(bf16)
        row_refs[slot][u, :, :size] = row_weights[:, :size]
        column_refs[slot][u] = column_weights
        spot_refs[slot][u, 0] = xr
        spot_refs[slot][u, 1] = qr
        spot_refs[slot][u, 2] = xc
        spot_refs[slot][u, 3] = qc

    def late(k, slot, u):
        row_leaf, column_leaf, _, _, _ = unpack(k, u)
        wr = row_refs[slot][u, :, :size]
        wc = column_refs[slot][u]
        column_sums = jnp.dot(
            jnp.concatenate([wr, wr], 1),
            cube_refs[slot][u, : 2 * size],
            preferred_element_type=f32,
        )
        row_sums = lax.dot_general(
            wc, cube_refs[slot][u, :size], turned, preferred_element_type=f32
        ) + lax.dot_general(
            wc, cube_refs[slot][u, size : 2 * size], turned, preferred_element_type=f32
        )
        row_field = field_of(padded(row_sums), spot_refs[slot][u, 0], spot_refs[slot][u, 1])
        column_field = field_of(column_sums, spot_refs[slot][u, 2], spot_refs[slot][u, 3])

        def store():
            field[row_leaf] = field[row_leaf] + row_field
            other_field[column_leaf] = other_field[column_leaf] + column_field

        return store

    pipeline(count, group, early, late)


def pair_scratch(group):
    return (
        [pltpu.VMEM((group, 2 * LEAF, LEAF), bf16)] * 2
        + [pltpu.VMEM((group, 32, LEAF), bf16)] * 2
        + [pltpu.VMEM((group, 32, LEAF), bf16)] * 2
        + [pltpu.VMEM((group, 4, 8, LEAF), f32)] * 2
    )


def paired(scratch):
    return [scratch[0:2], scratch[2:4], scratch[4:6], scratch[6:8]]


def front_kernel(place, send, send_p, spots, weights, up, bodies, moments, parents, *outs):
    def group_step(g, carry):
        rows = pl.ds(pl.multiple_of(8 * g, 8), 8)
        w = weights[rows, :]
        px = spots[0, rows, :]
        py = spots[1, rows, :]
        pz = spots[2, rows, :]
        for at, value in enumerate((w, px, py, pz)):
            bodies[pl.ds(64 * g + at, 8, stride=8), :] = value[:, :HALF]
            bodies[pl.ds(64 * g + 4 + at, 8, stride=8), :] = value[:, HALF:]
        cx = (place[0] + g // (CY * CZ // 8)).astype(f32) + 0.5
        cy = (place[1] + g // (CZ // 8) % CY).astype(f32) + 0.5
        base_z = (8 * (g % (CZ // 8))).astype(f32) + 0.5
        cz = row_ids((8, 1)).astype(f32) + base_z
        x, y, z = px - cx, py - cy, pz - cz
        table = {(0, 0, 0): w}
        axes = (x, y, z)
        lane = lane_ids((8, 128))
        built = jnp.zeros((8, 128), f32)
        for alpha in MULTI:
            if alpha not in table:
                lead = max(axis for axis in range(3) if alpha[axis])
                less = tuple(a - (axis == lead) for axis, a in enumerate(alpha))
                table[alpha] = table[less] * axes[lead]
            value = table[alpha]
            total = jnp.sum(value[:, :HALF] + value[:, HALF:], axis=1, keepdims=True)
            built = jnp.where(lane == PLACE[alpha], total, built)
        built = jnp.where(lane == CENTRE, cx, built)
        built = jnp.where(lane == CENTRE + 1, cy, built)
        built = jnp.where(lane == CENTRE + 2, cz, built)
        moments[rows, :] = built
        return carry

    lax.fori_loop(0, LEAVES // 8, group_step, 0, unroll=2)
    row = row_ids((8, HALF)) & 3
    bx = place[0].astype(f32) + 0.5
    by = place[1].astype(f32) + 0.5
    bodies[8 * LEAVES : 8 * LEAVES + 8, :] = jnp.where(
        row == 1, bx, jnp.where(row == 2, by, jnp.where(row == 3, 0.5, 0.0))
    )
    half_z = CZ // 2
    summed = jnp.zeros((PARENTS, 128), f32)
    for at in range(8):
        first = (at >> 2 & 1) * CY * CZ + (at >> 1 & 1) * CZ + (at & 1)
        piece = jnp.concatenate(
            [moments[pl.ds(first + 2 * CZ * py, half_z, stride=2), :] for py in range(CY // 2)], 0
        )
        summed = summed + jnp.dot(
            piece,
            up[128 * at : 128 * at + 128, :],
            precision=lax.Precision.HIGHEST,
            preferred_element_type=f32,
        )
    lane = lane_ids((PARENTS, 128))
    cell = row_ids((PARENTS, 128))
    summed = jnp.where(lane == CENTRE, place[0].astype(f32) + 1.0, summed)
    summed = jnp.where(
        lane == CENTRE + 1,
        place[1].astype(f32) + 1.0 + 2.0 * (cell // half_z).astype(f32),
        summed,
    )
    summed = jnp.where(lane == CENTRE + 2, 1.0 + 2.0 * (cell % half_z).astype(f32), summed)
    parents[...] = summed
    for way in range(4):

        def leaf_step(k, carry, way=way):
            leaf = send[0, way * SLOTS + k]
            outs[way][pl.ds(pl.multiple_of(8 * k, 8), 8), :] = bodies[
                pl.ds(pl.multiple_of(8 * leaf, 8), 8), :
            ]
            outs[way][pl.ds(BODY_ROWS + k, 1), :] = moments[pl.ds(leaf, 1), :]
            return carry

        lax.fori_loop(0, SLOTS, leaf_step, 0, unroll=8)

        def parent_step(k, carry, way=way):
            cell = send_p[0, way * PSLOTS + k]
            outs[way][pl.ds(BODY_ROWS + SLOTS + k, 1), :] = parents[pl.ds(cell, 1), :]
            return carry

        lax.fori_loop(0, PSLOTS, parent_step, 0, unroll=8)


def fill_tail(words, at, count, word, length):
    def step(k, carry):
        words[at, count + k] = word
        return carry

    lax.fori_loop(0, length, step, 0, unroll=8)


def self_kernel(place, counts, bodies, field, words, *scratch):
    field[...] = jnp.zeros_like(field)

    def sort_step(leaf, taken_so_far):
        short, long = taken_so_far
        is_short = counts[leaf] <= HALF
        at = jnp.where(is_short, 0, 1)
        words[at, jnp.where(is_short, short, long)] = leaf
        return jnp.where(is_short, short + 1, short), jnp.where(is_short, long, long + 1)

    short, long = lax.fori_loop(0, LEAVES, sort_step, (jnp.int32(0), jnp.int32(0)), unroll=8)
    fill_tail(words, 0, short, LEAVES, 3 * GROUP)
    fill_tail(words, 1, long, LEAVES, 3 * GROUP)
    refs = (scratch[0:2], scratch[2:4], scratch[4:6])
    self_loop(words, 0, short, GROUP, HALF, place, bodies, field, refs)
    self_loop(words, 1, long, GROUP, LEAF, place, bodies, field, refs)


def near_kernel(place, counts, pairs, bodies, field_in, field, words, *scratch):
    field[...] = field_in[...]

    def sort_step(k, taken_so_far):
        short, long = taken_so_far
        a = pairs[0, 0, k]
        b = pairs[0, 1, k]
        own = jnp.logical_and(b >= 0, b < LEAVES)
        b = jnp.where(own, b, 0)
        count_a = counts[a]
        count_b = counts[b]
        swapped = jnp.where(count_b < count_a, 1, 0)
        row_leaf = jnp.where(swapped == 1, b, a)
        column_leaf = jnp.where(swapped == 1, a, b)
        word = row_leaf | column_leaf << 9 | swapped << 18 | (pairs[0, 2, k] + 1) << 19 | 4 << 21
        is_short = jnp.minimum(count_a, count_b) <= HALF
        at = jnp.where(own, jnp.where(is_short, 0, 1), 2)
        words[at, jnp.where(is_short, short, long)] = word
        short = jnp.where(at == 0, short + 1, short)
        long = jnp.where(at == 1, long + 1, long)
        return short, long

    short, long = lax.fori_loop(
        0, pairs.shape[2], sort_step, (jnp.int32(0), jnp.int32(0)), unroll=8
    )
    empty = LEAVES << 9 | 1 << 19 | 4 << 21
    fill_tail(words, 0, short, empty, 3 * GROUP)
    fill_tail(words, 1, long, empty, 3 * GROUP)
    refs = paired(scratch)
    pair_loop(words, 0, short, GROUP, HALF, place, bodies, bodies, field, field, refs)
    pair_loop(words, 1, long, GROUP, LEAF, place, bodies, bodies, field, field, refs)


def derivatives(x, y, z):
    inverse = lax.rsqrt(x * x + y * y + z * z)
    square = inverse * inverse
    odd = [inverse]
    for _ in range(4):
        odd.append(odd[-1] * square)
    powers = monomials(x, y, z)
    result = {}
    for alpha in MULTI:
        degree = sum(alpha)
        total = None
        for p in range(alpha[0] // 2 + 1):
            for q in range(alpha[1] // 2 + 1):
                for s in range(alpha[2] // 2 + 1):
                    m = p + q + s
                    ways = math.prod(
                        math.factorial(a) // (2**c * math.factorial(c) * math.factorial(a - 2 * c))
                        for a, c in zip(alpha, (p, q, s))
                    )
                    sign = (-1.0) ** (degree - m)
                    double = math.prod(range(1, 2 * (degree - m), 2))
                    term = odd[degree - m] * (sign * double * ways)
                    rest = (alpha[0] - 2 * p, alpha[1] - 2 * q, alpha[2] - 2 * s)
                    if powers[rest] is not None:
                        term = term * powers[rest]
                    total = term if total is None else total + term
        result[alpha] = total
    return result


def remote_kernel(
    place,
    counts,
    pairs,
    far_a,
    far_b,
    far_lift,
    far_live,
    bodies,
    moments,
    parents,
    in_0,
    in_1,
    in_2,
    in_3,
    field_in,
    field,
    leaf_terms,
    parent_terms,
    out_0,
    out_1,
    out_2,
    out_3,
    words,
    far_bodies,
    far_field,
    gather_a,
    gather_b,
    *scratch,
):
    incoming = (in_0, in_1, in_2, in_3)
    outgoing = (out_0, out_1, out_2, out_3)
    field[...] = field_in[...]
    for way in range(4):
        far_bodies[way * SLOTS : (way + 1) * SLOTS] = incoming[way][:BODY_ROWS, :].reshape(
            SLOTS, 8, HALF
        )
    far_bodies[4 * SLOTS] = bodies[LEAVES]
    far_field[...] = jnp.zeros_like(far_field)

    def sort_step(k, taken_so_far):
        short, long = taken_so_far
        a = pairs[0, 0, k]
        b = pairs[0, 1, k]
        remote = b >= LEAVES
        b = jnp.maximum(b - LEAVES, 0)
        word = a | b << 9 | (pairs[0, 2, k] + 1) << 19 | (b // SLOTS) << 21
        is_short = counts[a] <= HALF
        at = jnp.where(remote, jnp.where(is_short, 0, 1), 2)
        words[at, jnp.where(is_short, short, long)] = word
        short = jnp.where(at == 0, short + 1, short)
        long = jnp.where(at == 1, long + 1, long)
        return short, long

    short, long = lax.fori_loop(
        0, pairs.shape[2], sort_step, (jnp.int32(0), jnp.int32(0)), unroll=8
    )
    empty = (4 * SLOTS) << 9 | 1 << 19 | 4 << 21
    fill_tail(words, 0, short, empty, 3 * GROUP)
    fill_tail(words, 1, long, empty, 3 * GROUP)
    refs = paired(scratch)
    group = GROUP // 2
    pair_loop(words, 0, short, group, HALF, place, bodies, far_bodies, field, far_field, refs)
    pair_loop(words, 1, long, group, LEAF, place, bodies, far_bodies, field, far_field, refs)
    for way in range(4):
        outgoing[way][:BODY_ROWS, :] = far_field[way * SLOTS : (way + 1) * SLOTS].reshape(
            BODY_ROWS, HALF
        )

    def moved(rows, way):
        lane = lane_ids(rows.shape)
        rows = jnp.where(lane == CENTRE, rows + place[2 + 2 * way].astype(f32), rows)
        return jnp.where(lane == CENTRE + 1, rows + place[3 + 2 * way].astype(f32), rows)

    table = [moments[...], parents[...]]
    for way in range(4):
        table.append(moved(incoming[way][BODY_ROWS : BODY_ROWS + SLOTS, :], way))
    for way in range(4):
        table.append(moved(incoming[way][BODY_ROWS + SLOTS :, :], way))
    table.append(jnp.zeros((ENTRIES - OWN - 4 * SLOTS - 4 * PSLOTS, 128), f32))
    columns = jnp.concatenate(table, 0).T[:FEATS]
    columns = jnp.concatenate(split3(columns), 0).astype(bf16)

    def one_hot(index, entries):
        return jnp.where(row_ids((entries, 128)) == index, 1.0, 0.0).astype(bf16)

    def joined(parts):
        return parts[:FEATS] + parts[FEATS : 2 * FEATS] + parts[2 * FEATS :]

    gather_a[...] = jnp.zeros_like(gather_a)
    gather_b[...] = jnp.zeros_like(gather_b)
    for block in range(FAR_BLOCKS):
        lanes = slice(128 * block, 128 * block + 128)
        rows = slice(FEATS * block, FEATS * block + FEATS)
        hot_a = one_hot(far_a[:, lanes], OWN)
        hot_b = one_hot(far_b[:, lanes], ENTRIES)
        gather_a[rows, :] = joined(jnp.dot(columns[:, :OWN], hot_a, preferred_element_type=f32))
        gather_b[rows, :] = joined(jnp.dot(columns, hot_b, preferred_element_type=f32))
    for chunk in range(2):
        start = 8 * chunk * FEATS

        def feature(ref, at, start=start):
            return ref[pl.ds(start + at, 8, stride=FEATS), :]

        def gap(axis):
            return feature(gather_a, CENTRE + axis) - feature(gather_b, CENTRE + axis)

        part = slice(8 * chunk, 8 * chunk + 8)
        live = far_live[part, :] > 0.0
        x = jnp.where(live, gap(0), 3.0)
        y = jnp.where(live, gap(1), 3.0)
        z = jnp.where(live, gap(2) - far_lift[part, :], 3.0)
        tensors = derivatives(x, y, z)
        held_a = {}
        held_b = {}
        for alpha in MULTI:
            held_a[alpha] = feature(gather_a, PLACE[alpha]) * (-1.0 / fact(alpha))
            held_b[alpha] = feature(gather_b, PLACE[alpha]) * (
                -((-1.0) ** sum(alpha)) / fact(alpha)
            )
        for beta in MULTI:
            to_a = None
            to_b = None
            for alpha in MULTI:
                if sum(alpha) + sum(beta) > 4:
                    continue
                tensor = tensors[added(alpha, beta)]
                term_a = held_b[alpha] * tensor
                term_b = held_a[alpha] * tensor
                to_a = term_a if to_a is None else to_a + term_a
                to_b = term_b if to_b is None else to_b + term_b
            if sum(beta) % 2:
                to_b = -to_b
            gather_a[pl.ds(start + PLACE[beta], 8, stride=FEATS), :] = to_a
            gather_b[pl.ds(start + PLACE[beta], 8, stride=FEATS), :] = to_b
    sums_a = jnp.zeros((3 * FEATS, OWN), f32)
    sums_b = jnp.zeros((3 * FEATS, ENTRIES), f32)
    turned = (((1,), (1,)), ((), ()))
    for block in range(FAR_BLOCKS):
        lanes = slice(128 * block, 128 * block + 128)
        rows = slice(FEATS * block, FEATS * block + FEATS)
        parts_a = jnp.concatenate(split3(gather_a[rows, :]), 0).astype(bf16)
        parts_b = jnp.concatenate(split3(gather_b[rows, :]), 0).astype(bf16)
        hot_a = one_hot(far_a[:, lanes], OWN)
        hot_b = one_hot(far_b[:, lanes], ENTRIES)
        sums_a = sums_a + lax.dot_general(parts_a, hot_a, turned, preferred_element_type=f32)
        sums_b = sums_b + lax.dot_general(parts_b, hot_b, turned, preferred_element_type=f32)
    got_a = jnp.concatenate([joined(sums_a), jnp.zeros((128 - FEATS, OWN), f32)], 0)
    got_b = jnp.concatenate([joined(sums_b), jnp.zeros((128 - FEATS, ENTRIES), f32)], 0)
    keep = lane_ids((1, 128)) < TERMS
    terms_a = jnp.where(keep, got_a.T, 0.0)
    terms_b = jnp.where(keep, got_b.T, 0.0)
    leaf_terms[...] = terms_a[:LEAVES] + terms_b[:LEAVES]
    parent_terms[...] = terms_a[LEAVES:OWN] + terms_b[LEAVES:OWN]
    leaf_start = OWN
    parent_start = OWN + 4 * SLOTS
    for way in range(4):
        first = leaf_start + way * SLOTS
        outgoing[way][BODY_ROWS : BODY_ROWS + SLOTS, :] = terms_b[first : first + SLOTS]
        first = parent_start + way * PSLOTS
        outgoing[way][BODY_ROWS + SLOTS :, :] = terms_b[first : first + PSLOTS]


def back_kernel(
    place,
    counts,
    send,
    send_p,
    spots,
    field_in,
    leaf_in,
    parent_in,
    down,
    in_0,
    in_1,
    in_2,
    in_3,
    out,
    leaf_terms,
    parent_terms,
    field,
    tiles,
):
    incoming = (in_0, in_1, in_2, in_3)
    leaf_terms[...] = leaf_in[...]
    parent_terms[...] = parent_in[...]
    field[...] = field_in[...]
    for way in range(4):

        def leaf_step(k, carry, way=way):
            leaf = send[0, way * SLOTS + k]
            field[leaf] = field[leaf] + incoming[way][pl.ds(pl.multiple_of(8 * k, 8), 8), :]
            leaf_terms[pl.ds(leaf, 1), :] = (
                leaf_terms[pl.ds(leaf, 1), :] + incoming[way][pl.ds(BODY_ROWS + k, 1), :]
            )
            return carry

        lax.fori_loop(0, SLOTS, leaf_step, 0, unroll=8)

        def parent_step(k, carry, way=way):
            cell = send_p[0, way * PSLOTS + k]
            parent_terms[pl.ds(cell, 1), :] = (
                parent_terms[pl.ds(cell, 1), :] + incoming[way][pl.ds(BODY_ROWS + SLOTS + k, 1), :]
            )
            return carry

        lax.fori_loop(0, PSLOTS, parent_step, 0, unroll=8)
    half_z = CZ // 2
    for at in range(8):
        moved = jnp.dot(
            parent_terms[...],
            down[:, 128 * at : 128 * at + 128],
            precision=lax.Precision.HIGHEST,
            preferred_element_type=f32,
        )
        first = (at >> 2 & 1) * CY * CZ + (at >> 1 & 1) * CZ + (at & 1)
        for py in range(CY // 2):
            rows = pl.ds(first + 2 * CZ * py, half_z, stride=2)
            leaf_terms[rows, :] = leaf_terms[rows, :] + moved[half_z * py : half_z * py + half_z]

    def group_step(g, carry):
        rows = pl.ds(pl.multiple_of(8 * g, 8), 8)
        cx = (place[0] + g // (CY * CZ // 8)).astype(f32) + 0.5
        cy = (place[1] + g // (CZ // 8) % CY).astype(f32) + 0.5
        base_z = (8 * (g % (CZ // 8))).astype(f32) + 0.5
        cz = row_ids((8, 1)).astype(f32) + base_z
        x = spots[0, rows, :] - cx
        y = spots[1, rows, :] - cy
        z = spots[2, rows, :] - cz
        terms = leaf_terms[rows, :]
        powers = monomials(x, y, z)
        column = {
            alpha: jnp.broadcast_to(terms[:, PLACE[alpha] : PLACE[alpha] + 1], (8, LEAF))
            for alpha in MULTI
        }
        totals = [None] * 4
        for beta in MULTI:
            scale = 1.0 / fact(beta)
            base = powers[beta]
            if base is not None and scale != 1.0:
                base = base * scale
            kinds = [beta] + (
                [added(beta, unit) for unit in ((1, 0, 0), (0, 1, 0), (0, 0, 1))]
                if sum(beta) < 4
                else []
            )
            for at, kind in enumerate(kinds):
                term = column[kind] if base is None else column[kind] * base
                totals[at] = term if totals[at] is None else totals[at] + term
        values = [totals[0], -totals[1], -totals[2], -totals[3]]
        for at, value in enumerate(values):
            tiles[pl.ds(at, 8, stride=8), :] = value[:, :HALF]
            tiles[pl.ds(4 + at, 8, stride=8), :] = value[:, HALF:]
        row = row_ids((8, HALF))
        body = lane_ids((8, HALF)) + jnp.where(row < 4, 0, HALF)
        for u in range(8):
            leaf = 8 * g + u
            tile = tiles[8 * u : 8 * u + 8, :] + field[leaf]
            tile = jnp.where(body < counts[leaf], tile, 0.0)
            start = pl.multiple_of(leaf * LEAF, LEAF)
            out[:, pl.ds(start, HALF)] = tile[:4]
            out[:, pl.ds(start + HALF, HALF)] = tile[4:]
        return carry

    lax.fori_loop(0, LEAVES // 8, group_step, 0)


VMEM = pl.BlockSpec(memory_space=pltpu.VMEM)
SMEM = pl.BlockSpec(memory_space=pltpu.SMEM)
params = pltpu.CompilerParams(vmem_limit_bytes=56 * 1024 * 1024)
packed = jax.ShapeDtypeStruct((PACK_ROWS, 128), f32)
tiled = jax.ShapeDtypeStruct((LEAVES + 1, 8, HALF), f32)


def shaped(*dims):
    return jax.ShapeDtypeStruct(dims, f32)


def on_device(
    positions, masses, leaf_counts, send_leaves, send_parents, near_pairs, far_pairs, parent_pairs
):
    slab_count = lax.axis_size("slab")
    sub_count = lax.axis_size("sub")
    slab_at = lax.axis_index("slab")
    sub_at = lax.axis_index("sub")
    spots = positions.reshape(3, LEAVES, LEAF)
    filled = lax.broadcasted_iota(i32, (LEAVES, LEAF), 1) < leaf_counts[:, None]
    weights = jnp.where(filled, masses.reshape(LEAVES, LEAF), 0.0)
    numbers = [slab_at * CX, sub_at * CY]
    for way in range(4):
        reach_x = slab_at + slab_steps[way]
        reach_y = sub_at + sub_steps[way]
        numbers.append((reach_x - reach_x % slab_count) * CX)
        numbers.append((reach_y - reach_y % sub_count) * CY)
    zero = jnp.zeros((), i32)
    place = jnp.stack(numbers + [zero] * 6).astype(i32)

    sent = pl.pallas_call(
        front_kernel,
        out_shape=[shaped(8 * LEAVES + 8, HALF), shaped(LEAVES, 128), shaped(PARENTS, 128)]
        + [packed] * 4,
        in_specs=[SMEM, SMEM, SMEM, VMEM, VMEM, VMEM],
        out_specs=[VMEM] * 7,
        compiler_params=params,
        name="moments_and_packing",
    )(place, send_leaves, send_parents, spots, weights, jnp.asarray(UP))
    bodies = sent[0].reshape(LEAVES + 1, 8, HALF)
    moments, parents = sent[1], sent[2]

    def exchange(value, way, back):
        pairs = []
        for s in range(slab_count):
            for u in range(sub_count):
                here = s * sub_count + u
                there = (s + slab_steps[way]) % slab_count * sub_count + (
                    u + sub_steps[way]
                ) % sub_count
                pairs.append((here, there) if back else (there, here))
        return lax.ppermute(value, ("slab", "sub"), pairs)

    incoming = [exchange(sent[3 + way], way, False) for way in range(4)]

    field = pl.pallas_call(
        self_kernel,
        out_shape=tiled,
        in_specs=[SMEM, SMEM, VMEM],
        out_specs=VMEM,
        scratch_shapes=[pltpu.SMEM((2, LEAVES + 4 * GROUP), i32)]
        + [pltpu.VMEM((GROUP, 2 * LEAF, LEAF), bf16)] * 2
        + [pltpu.VMEM((GROUP, 32, LEAF), bf16)] * 2
        + [pltpu.VMEM((GROUP, 2, 8, LEAF), f32)] * 2,
        compiler_params=params,
        cost_estimate=pl.CostEstimate(
            flops=20_000_000_000, bytes_accessed=2_000_000, transcendentals=0
        ),
        name="self_pairs",
    )(place, leaf_counts, bodies)

    def far_row(leaf_part, parent_part, fill):
        count = FAR_BLOCKS * 128 - leaf_part.shape[0] - parent_part.shape[0]
        return jnp.concatenate([leaf_part, parent_part, jnp.full((count,), fill, leaf_part.dtype)])

    far = far_pairs[0]
    cells = parent_pairs[0]
    far_on = far[1] >= 0
    cells_on = cells[1] >= 0
    index_a = far_row(jnp.where(far_on, far[0], -1), jnp.where(cells_on, cells[0] + LEAVES, -1), -1)
    index_b = far_row(
        jnp.where(far[1] >= LEAVES, far[1] + PARENTS, far[1]),
        jnp.where(
            cells_on,
            jnp.where(
                cells[1] >= PARENTS, cells[1] + (OWN + 4 * SLOTS - PARENTS), cells[1] + LEAVES
            ),
            -1,
        ),
        -1,
    )
    index_a = index_a.reshape(1, -1)
    index_b = index_b.reshape(1, -1)
    spare = jnp.zeros((16 * 128 - FAR_BLOCKS * 128,), f32)
    lifts = far_row(far[2] * CZ, cells[2] * CZ, 0).astype(f32)
    lifts = jnp.concatenate([lifts, spare]).reshape(16, 128)
    live = far_row(far_on.astype(f32), cells_on.astype(f32), 0.0)
    live = jnp.concatenate([live, spare]).reshape(16, 128)

    middle = pl.pallas_call(
        remote_kernel,
        out_shape=[tiled, shaped(LEAVES, 128), shaped(PARENTS, 128)] + [packed] * 4,
        in_specs=[SMEM] * 3 + [VMEM] * 12,
        out_specs=[VMEM] * 7,
        scratch_shapes=[
            pltpu.SMEM((3, near_pairs.shape[2] + 4 * GROUP), i32),
            pltpu.VMEM((4 * SLOTS + 1, 8, HALF), f32),
            pltpu.VMEM((4 * SLOTS + 1, 8, HALF), f32),
            pltpu.VMEM((16 * FEATS, 128), f32),
            pltpu.VMEM((16 * FEATS, 128), f32),
        ]
        + pair_scratch(GROUP // 2),
        compiler_params=params,
        name="pairs_with_others",
    )(
        place,
        leaf_counts,
        near_pairs,
        index_a,
        index_b,
        lifts,
        live,
        bodies,
        moments,
        parents,
        *incoming,
        field,
    )
    field, leaf_terms, parent_terms = middle[:3]
    arrived = [exchange(middle[3 + way], way, True) for way in range(4)]

    field = pl.pallas_call(
        near_kernel,
        out_shape=tiled,
        in_specs=[SMEM] * 3 + [VMEM] * 2,
        out_specs=VMEM,
        scratch_shapes=[pltpu.SMEM((3, near_pairs.shape[2] + 4 * GROUP), i32)]
        + pair_scratch(GROUP),
        compiler_params=params,
        cost_estimate=pl.CostEstimate(
            flops=20_000_000_000, bytes_accessed=2_000_000, transcendentals=0
        ),
        name="own_pairs",
    )(place, leaf_counts, near_pairs, bodies, field)

    return pl.pallas_call(
        back_kernel,
        out_shape=jax.ShapeDtypeStruct((4, LEAVES * LEAF), f32),
        in_specs=[SMEM] * 4 + [VMEM] * 9,
        out_specs=VMEM,
        scratch_shapes=[
            pltpu.VMEM((LEAVES, 128), f32),
            pltpu.VMEM((PARENTS, 128), f32),
            pltpu.VMEM((LEAVES + 1, 8, HALF), f32),
            pltpu.VMEM((64, HALF), f32),
        ],
        compiler_params=params,
        name="shift_and_evaluate",
    )(
        place,
        leaf_counts,
        send_leaves,
        send_parents,
        spots,
        field,
        leaf_terms,
        parent_terms,
        jnp.asarray(DOWN),
        *arrived,
    )


def solution(mesh):
    return jax.shard_map(
        on_device,
        mesh=mesh,
        in_specs=(
            P(None, ("slab", "sub")),
            P(("slab", "sub")),
            P(("slab", "sub")),
            P(("slab", "sub"), None),
            P(("slab", "sub"), None),
            P(("slab", "sub"), None, None),
            P(("slab", "sub"), None, None),
            P(("slab", "sub"), None, None),
        ),
        out_specs=P(None, ("slab", "sub")),
        check_vma=False,
    )
```

time: 868 us -> 119 us (0.14)
  the two profiles are of different devices: /device:TPU:0 before, /device:TPU:1 now
where the time goes in v1:
time: 119 us; the launch traced here: 118 us
  Pallas kernels  90.1 us (76%)
  starting transfers between devices  17.3 us (15%)
  local copies, waits for them, and re-layouts  9.22 us (8%)
    pallas_call x1, Pallas kernels, on_device(): pl.pallas_call(near_kernel, out_shape=tiled, in_specs=[SMEM] * 3 + [VMEM]...  30.7 us
    pallas_call x1, Pallas kernels, on_device(): pl.pallas_call(self_kernel, out_shape=tiled, in_specs=[SMEM, SMEM, VMEM],...  27.3 us
    ppermute x8, starting transfers between devices, exchange(): return lax.ppermute(value, ('slab', 'sub'), pairs)  17.3 us
    pallas_call x1, Pallas kernels, on_device(): pl.pallas_call(remote_kernel, out_shape=[tiled, shaped(LEAVES, 128), shap...  15.2 us
    pallas_call x1, Pallas kernels, on_device(): pl.pallas_call(back_kernel, out_shape=jax.ShapeDtypeStruct((4, LEAVES * L...  9.96 us
    pallas_call x1, Pallas kernels, on_device(): pl.pallas_call(front_kernel, out_shape=[shaped(8 * LEAVES + 8, HALF), sha...  6.92 us
    unnamed x26, local copies, waits for them, and re-layouts  4.87 us
  transfers between devices with their start and end apart: 8, of which 0 were waited for; matrix products, arithmetic and copies ran while one was open for 3% of the time, Pallas kernels for 49%

profile of v1, /device:TPU:1, one launch (start us, length us, event | category | flops | bytes accessed | tf_op | source)
XLA Modules:
  0.0 117.6 jit_solution(10513838985127580344)
XLA Ops:
  0.0 1.0 reshape.56
  1.0 2.3 %copy.15 = f32[1,3,256,256]{3,2,1,0:T(8,128)} copy(f32[1,3,256,256]{3,1,2,0:T(4,128)} %bitcast.31) | data formatting | bytes 1572864
  3.3 0.8 fusion.weights
  4.1 0.6 stack.34.place
  4.8 6.9 %moments_and_packing.1 = (f32[2056,128]{1,0:T(8,128)}, f32[256,128]{1,0:T(8,128)}, f32[32,128]{1,0:T(8,128)}, f32[592,128]{1,0:T(8,128)}, f32[592,128]{1,0:T(8,1...) custom-call(s32[16]{0:T(128)} %stack.34.place, s32[1,256]{1,0:T(1,128)} %send.3, s32[1,64]{1,0:T(1,128)} %send_p.3, ...), custom_call_target="tpu_custom_call" | custom-call | tf_op jit(solution)/shard_map/moments_and_packing/pallas_call | solution.py:787
  11.8 5.7 %collective-permute-start.1 = (f32[592,128]{1,0:T(8,128)}, f32[592,128]{1,0:T(8,128)S(1)}, u32[]{:S(2)}, u32[]{:S(2)}) collective-permute-start(f32[592,128]{1,0:T(8,128)} %get-tuple-element.23), channel_id=1, source_target_pairs={{1,0},{2,1},{3,2},{4,3},{5,4},{6,5},{7,6},{0,7},{9,8},{10,9},{11,1... | collective-permute-start | bytes 909320 | tf_op jit(solution)/shard_map/ppermute | solution.py:808
  17.4 1.4 %collective-permute-start.2 = (f32[592,128]{1,0:T(8,128)}, f32[592,128]{1,0:T(8,128)S(1)}, u32[]{:S(2)}, u32[]{:S(2)}) collective-permute-start(f32[592,128]{1,0:T(8,128)} %get-tuple-element.24), channel_id=1, source_target_pairs={{9,0},{10,1},{11,2},{12,3},{13,4},{14,5},{15,6},{8,7},{17,8},{18,9... | collective-permute-start | bytes 909320 | tf_op jit(solution)/shard_map/ppermute | solution.py:808
  18.8 1.3 %collective-permute-start.3 = (f32[592,128]{1,0:T(8,128)}, f32[592,128]{1,0:T(8,128)S(1)}, u32[]{:S(2)}, u32[]{:S(2)}) collective-permute-start(f32[592,128]{1,0:T(8,128)} %get-tuple-element.25), channel_id=1, source_target_pairs={{15,0},{8,1},{9,2},{10,3},{11,4},{12,5},{13,6},{14,7},{23,8},{16,9... | collective-permute-start | bytes 909320 | tf_op jit(solution)/shard_map/ppermute | solution.py:808
  20.2 0.6 copy.12.pairs
  21.0 0.6 reshape.58.far_a
  21.7 0.6 reshape.59.far_b
  22.2 27.3 %self_pairs.1.field_in = f32[257,8,128]{2,1,0:T(8,128)} custom-call(s32[16]{0:T(128)} %stack.34.place, s32[256]{0:T(256)} %counts.7, f32[257,8,128]{2,1,0:T(8,128)} %bitcast.28), custom_call_target="tpu_custom_call" | custom-call | flops 20000000000 | bytes 2000000 | tf_op jit(solution)/shard_map/self_pairs/pallas_call | solution.py:812
  49.5 0.7 concatenate.19
  50.2 0.6 pad_bitcast_fusion.far_lift
  50.8 0.7 copy-done.4
  51.5 0.1 copy-done.5
  51.8 15.2 %pairs_with_others.1 = (f32[257,8,128]{2,1,0:T(8,128)}, f32[256,128]{1,0:T(8,128)}, f32[32,128]{1,0:T(8,128)}, f32[592,128]{1,0:T(8,128)}, f32[592,128]{1,0:T(8,...) custom-call(s32[16]{0:T(128)} %stack.34.place, s32[256]{0:T(256)} %counts.7, s32[1,3,256]{2,1,0:T(4,128)} %copy.12.pairs, ...), custom_call_target="tpu_custom_call" | custom-call | tf_op jit(solution)/shard_map/pairs_with_others/pallas_call | solution.py:856
  67.0 4.6 %collective-permute-start.4 = (f32[592,128]{1,0:T(8,128)}, f32[592,128]{1,0:T(8,128)S(1)}, u32[]{:S(2)}, u32[]{:S(2)}) collective-permute-start(f32[592,128]{1,0:T(8,128)} %get-tuple-element.29), channel_id=1, source_target_pairs={{0,8},{1,9},{2,10},{3,11},{4,12},{5,13},{6,14},{7,15},{8,16},{9,17... | collective-permute-start | bytes 909320 | tf_op jit(solution)/shard_map/ppermute | solution.py:808
  71.6 4.2 %collective-permute-start.7 = (f32[592,128]{1,0:T(8,128)}, f32[592,128]{1,0:T(8,128)S(1)}, u32[]{:S(2)}, u32[]{:S(2)}) collective-permute-start(f32[592,128]{1,0:T(8,128)} %get-tuple-element.32), channel_id=1, source_target_pairs={{0,15},{1,8},{2,9},{3,10},{4,11},{5,12},{6,13},{7,14},{8,23},{9,16... | collective-permute-start | bytes 909320 | tf_op jit(solution)/shard_map/ppermute | solution.py:808
  75.8 30.7 %own_pairs.1.field_in = f32[257,8,128]{2,1,0:T(8,128)} custom-call(s32[16]{0:T(128)} %stack.34.place, s32[256]{0:T(256)} %counts.7, s32[1,3,256]{2,1,0:T(4,128)} %copy.12.pairs, f32[257,8,128]{2,1,0:T(8,128)} %bitcast.30, f32[257,8,128]{2,1,0:T(8,128)} %get-tuple-element.26.field_in), custom_call_target="tpu_custom_call" | custom-call | flops 20000000000 | bytes 2000000 | tf_op jit(solution)/shard_map/own_pairs/pallas_call | solution.py:888
  106.6 0.7 copy-done
  107.3 0.1 copy-done.1
  107.5 0.1 copy-done.3
  107.6 10.0 %shift_and_evaluate.1 = f32[4,65536]{1,0:T(4,128)} custom-call(s32[16]{0:T(128)} %stack.34.place, s32[256]{0:T(256)} %counts.7, s32[1,256]{1,0:T(1,128)} %send.3, s32[1,64]{1,0:T(1,128)} %send_p.3, f32[3,256,256]{2,1,0:T(8,128)} %bitcast.27, f32[257,8,128]{2,1,0:T(8,128)} %own_pairs.1.field_in, f32[256,128]{1,0:T(8,128)} %get-tuple-element.27.leaf_in, ...), custom_call_target="tpu_custom_call" | custom-call | tf_op jit(solution)/shard_map/shift_and_evaluate/pallas_call | solution.py:902
  (46 shorter events, 0.7 us)
Async XLA Ops:
  0.0 3.3 %copy-start.9 = (s32[256]{0:T(256)S(1)}, s32[256]{0:T(256)}, u32[]{:S(2)}) copy-start(s32[256]{0:T(256)} %counts.7) | copy-start | bytes 3076
  3.3 16.8 %copy-start.8 = (s32[1,3,1024]{2,0,1:T(1,128)S(1)}, s32[1,3,1024]{2,0,1:T(1,128)}, u32[]{:S(2)}) copy-start(s32[1,3,1024]{2,0,1:T(1,128)} %param.16) | copy-start | bytes 36868
  3.3 16.9 %copy-start.11 = (s32[1,3,64]{2,0,1:T(1,128)S(1)}, s32[1,3,64]{2,0,1:T(1,128)}, u32[]{:S(2)}) copy-start(s32[1,3,64]{2,0,1:T(1,128)} %param.17) | copy-start | bytes 2308
  3.3 16.9 %copy-start.10 = (s32[1,3,256]{2,0,1:T(1,128)S(1)}, s32[1,3,256]{2,0,1:T(1,128)}, u32[]{:S(2)}) copy-start(s32[1,3,256]{2,0,1:T(1,128)} %param.15) | copy-start | bytes 9220
  11.7 39.1 %collective-permute-start = (f32[592,128]{1,0:T(8,128)}, f32[592,128]{1,0:T(8,128)S(1)}, u32[]{:S(2)}, u32[]{:S(2)}) collective-permute-start(f32[592,128]{1,0:T(8,128)} %get-tuple-element.22), channel_id=1, source_target_pairs={{8,0},{9,1},{10,2},{11,3},{12,4},{13,5},{14,6},{15,7},{16,8},{17,9... | collective-permute-start | bytes 909320 | tf_op jit(solution)/shard_map/ppermute | solution.py:808
  11.8 39.0 %collective-permute-start.1 = (f32[592,128]{1,0:T(8,128)}, f32[592,128]{1,0:T(8,128)S(1)}, u32[]{:S(2)}, u32[]{:S(2)}) collective-permute-start(f32[592,128]{1,0:T(8,128)} %get-tuple-element.23), channel_id=1, source_target_pairs={{1,0},{2,1},{3,2},{4,3},{5,4},{6,5},{7,6},{0,7},{9,8},{10,9},{11,1... | collective-permute-start | bytes 909320 | tf_op jit(solution)/shard_map/ppermute | solution.py:808
  17.4 33.4 %collective-permute-start.2 = (f32[592,128]{1,0:T(8,128)}, f32[592,128]{1,0:T(8,128)S(1)}, u32[]{:S(2)}, u32[]{:S(2)}) collective-permute-start(f32[592,128]{1,0:T(8,128)} %get-tuple-element.24), channel_id=1, source_target_pairs={{9,0},{10,1},{11,2},{12,3},{13,4},{14,5},{15,6},{8,7},{17,8},{18,9... | collective-permute-start | bytes 909320 | tf_op jit(solution)/shard_map/ppermute | solution.py:808
  18.8 32.0 %collective-permute-start.3 = (f32[592,128]{1,0:T(8,128)}, f32[592,128]{1,0:T(8,128)S(1)}, u32[]{:S(2)}, u32[]{:S(2)}) collective-permute-start(f32[592,128]{1,0:T(8,128)} %get-tuple-element.25), channel_id=1, source_target_pairs={{15,0},{8,1},{9,2},{10,3},{11,4},{12,5},{13,6},{14,7},{23,8},{16,9... | collective-permute-start | bytes 909320 | tf_op jit(solution)/shard_map/ppermute | solution.py:808
  50.8 0.7 copy-start.4
  50.8 0.8 copy-start.5
  50.8 0.9 copy-start.6
  50.8 1.0 copy-start.7
  67.0 39.6 %collective-permute-start.4 = (f32[592,128]{1,0:T(8,128)}, f32[592,128]{1,0:T(8,128)S(1)}, u32[]{:S(2)}, u32[]{:S(2)}) collective-permute-start(f32[592,128]{1,0:T(8,128)} %get-tuple-element.29), channel_id=1, source_target_pairs={{0,8},{1,9},{2,10},{3,11},{4,12},{5,13},{6,14},{7,15},{8,16},{9,17... | collective-permute-start | bytes 909320 | tf_op jit(solution)/shard_map/ppermute | solution.py:808
  71.6 35.0 %collective-permute-start.5 = (f32[592,128]{1,0:T(8,128)}, f32[592,128]{1,0:T(8,128)S(1)}, u32[]{:S(2)}, u32[]{:S(2)}) collective-permute-start(f32[592,128]{1,0:T(8,128)} %get-tuple-element.30), channel_id=1, source_target_pairs={{0,1},{1,2},{2,3},{3,4},{4,5},{5,6},{6,7},{7,0},{8,9},{9,10},{10,1... | collective-permute-start | bytes 909320 | tf_op jit(solution)/shard_map/ppermute | solution.py:808
  71.6 35.0 %collective-permute-start.6 = (f32[592,128]{1,0:T(8,128)}, f32[592,128]{1,0:T(8,128)S(1)}, u32[]{:S(2)}, u32[]{:S(2)}) collective-permute-start(f32[592,128]{1,0:T(8,128)} %get-tuple-element.31), channel_id=1, source_target_pairs={{0,9},{1,10},{2,11},{3,12},{4,13},{5,14},{6,15},{7,8},{8,17},{9,18... | collective-permute-start | bytes 909320 | tf_op jit(solution)/shard_map/ppermute | solution.py:808
  71.6 35.0 %collective-permute-start.7 = (f32[592,128]{1,0:T(8,128)}, f32[592,128]{1,0:T(8,128)S(1)}, u32[]{:S(2)}, u32[]{:S(2)}) collective-permute-start(f32[592,128]{1,0:T(8,128)} %get-tuple-element.32), channel_id=1, source_target_pairs={{0,15},{1,8},{2,9},{3,10},{4,11},{5,12},{6,13},{7,14},{8,23},{9,16... | collective-permute-start | bytes 909320 | tf_op jit(solution)/shard_map/ppermute | solution.py:808
  106.6 0.7 copy-start
  106.6 0.8 copy-start.1
  106.6 0.9 copy-start.2
  106.6 1.0 copy-start.3
